TPU v7x, 32 devices: a whole 2x2x4 slice. The times are simulated.
32 devices in a mesh: grp: 2 (over x), lon: 16 (over z, y, core).
Axes of the slice: x: 2, y: 2, z: 4, core: 2. Of those that a mesh axis runs over, the one named last changes fastest.
Arguments:
- fields: bfloat16 [1024, 16, 1440], P(('grp', 'lon')), parts along dimension 0, may hold values from -6 to 6
- filter_basis: bfloat16 [16, 3, 6, 32, 96], P('lon'), may hold values from -0.4375 to 0.4375
- offsets: int32 [16, 6], P('lon'), may hold values from 0 to 44, as said below
- counts: int32 [16], P('lon'), may hold values from 1 to 6
- mixing: bfloat16 [512, 1536], replicated, may hold values from -0.15625 to 0.15625
- cotangent: bfloat16 [1024, 16, 1440], P('grp', 'lon'), parts along dimension 0, may hold values from -6 to 6
Outputs:
- mixed_out: bfloat16 [1024, 16, 1440], P('grp', 'lon'), parts along dimension 0
- field_grad: bfloat16 [1024, 16, 1440], P(('grp', 'lon')), parts along dimension 0
- mixing_grad: float32 [1024, 1536], P(('grp', 'lon')), parts along dimension 0
There are 2 independent parts, one for each index of `grp`. A program takes and returns all parts, laid end to end along the dimension named above; an argument that names none is the same for every part. Nothing has to cross between parts.
Inputs may be any that keep to these rules, and one draw needn't show every extreme that they name: The 6 block offsets of a row are distinct.
All inputs are finite; a program needn't handle non-finite values.
Results may differ from a plain program's by a relative error of at most 0.006.
Values may be sent and summed in bfloat16 or wider, within the bound.
A program may use at most 128 MiB of HBM per device.

v0:
```python
import jax
import jax.numpy as jnp
from jax import lax
from jax.sharding import PartitionSpec as P


def extended_2(block, sides, width):
    for axis, dim in sides:
        count = lax.axis_size(axis)
        forward = [(i, i + 1) for i in range(count - 1)]
        backward = [(target, source) for source, target in forward]
        low = lax.ppermute(
            lax.slice_in_dim(block, block.shape[dim] - width, None, axis=dim), axis, forward
        )
        high = lax.ppermute(lax.slice_in_dim(block, 0, width, axis=dim), axis, backward)
        block = jnp.concatenate([low, block, high], axis=dim)
    return block


def passed_along(value, axis, steps):
    count = lax.axis_size(axis)
    leading, last = (max(0, -steps), min(count, count - steps))
    return lax.ppermute(value, axis, [(source, source + steps) for source in range(leading, last)])


def slot_weights(filter_basis, row_index):
    weights = filter_basis[row_index]
    slots = weights.shape[1]
    block = weights.shape[2]
    outer = weights.shape[3]
    return weights.transpose(1, 0, 2, 3).reshape(slots, 3 * block, outer)


def contract(extended, filter_basis, offsets, counts):
    channels = extended.shape[0]
    height = extended.shape[1]
    width = extended.shape[2]
    rows = filter_basis.shape[0]
    block = filter_basis.shape[3]
    outer = filter_basis.shape[4]
    nblocks = width // block
    kernels = outer // block
    blocked = extended.reshape(channels, height, nblocks, block).transpose(2, 0, 1, 3)

    def contract_one_row(row_index):
        window = blocked.reshape(nblocks, channels, 3 * block)
        weights = slot_weights(filter_basis, row_index)
        offset_row = offsets[row_index]
        live = counts[row_index]

        def contract_slot_term(slot, piece):
            shifted = jnp.roll(window, -offset_row[slot], axis=0)
            return jnp.einsum("bcx,xy->bcy", shifted, piece, preferred_element_type=jnp.float32)

        def contract_add_slot(slot, total):
            piece = lax.dynamic_index_in_dim(weights, slot, 0, keepdims=False)
            return total + contract_slot_term(slot, piece)

        total = lax.fori_loop(
            0, live, contract_add_slot, jnp.zeros((nblocks, channels, outer), jnp.float32)
        )
        return total

    mapped = lax.map(contract_one_row, jnp.arange(rows, dtype=jnp.int32))
    mapped = mapped.reshape(rows, nblocks, channels, kernels, block)
    return mapped.transpose(2, 3, 0, 1, 4).reshape(channels, kernels, rows, width)


def adjoint(grads, filter_basis, offsets, counts):
    channels = grads.shape[0]
    width = grads.shape[3]
    rows = filter_basis.shape[0]
    block = filter_basis.shape[3]
    outer = filter_basis.shape[4]
    nblocks = width // block
    kernels = outer // block
    blocked = (
        grads.reshape(channels, kernels, rows, nblocks, block)
        .transpose(2, 3, 0, 1, 4)
        .reshape(rows, nblocks, channels, outer)
    )

    def adjoint_one_row(row_index):
        row = blocked[row_index]
        weights = slot_weights(filter_basis, row_index)
        offset_row = offsets[row_index]
        live = counts[row_index]

        def adjoint_slot_term(slot, piece):
            term = jnp.einsum("bcy,xy->bcx", row, piece, preferred_element_type=jnp.float32)
            return jnp.roll(term, offset_row[slot], axis=0)

        def adjoint_add_slot(slot, total):
            piece = lax.dynamic_index_in_dim(weights, slot, 0, keepdims=False)
            return total + adjoint_slot_term(slot, piece)

        total = lax.fori_loop(
            0, live, adjoint_add_slot, jnp.zeros((nblocks, channels, 3 * block), jnp.float32)
        )
        return total

    mapped = lax.map(adjoint_one_row, jnp.arange(rows, dtype=jnp.int32))
    mapped = (
        mapped.reshape(rows, nblocks, channels, 3, block)
        .transpose(2, 3, 0, 1, 4)
        .reshape(channels, 3, rows, width)
    )
    spread = jnp.zeros((channels, rows + 2, width), jnp.float32)
    for shift_rows in range(3):
        spread = spread + jnp.pad(
            mapped[:, shift_rows], ((0, 0), (shift_rows, 2 - shift_rows), (0, 0))
        )
    return spread


def local(fields, filter_basis, offsets, counts, mixing, cotangent):
    kernels = mixing.shape[1] // mixing.shape[0]
    own_rows = lax.all_to_all(fields, "lon", split_axis=1, concat_axis=0, tiled=True)
    extended = extended_2(own_rows, (("lon", 1),), 1)
    features = contract(extended, filter_basis, offsets, counts).astype(jnp.bfloat16)
    channels = own_rows.shape[0]
    rows = own_rows.shape[1]
    width = own_rows.shape[2]
    flat = features.reshape(channels * kernels, rows, width)
    mixed = jnp.einsum("om,mrp->orp", mixing, flat, preferred_element_type=jnp.float32)
    mixed_out = (own_rows.astype(jnp.float32) + mixed).astype(jnp.bfloat16)
    mixing_grad = lax.psum_scatter(
        jnp.einsum("orp,mrp->om", cotangent, flat, preferred_element_type=jnp.float32),
        "lon",
        scatter_dimension=0,
        tiled=True,
    )
    feature_grad = jnp.einsum(
        "om,orp->mrp", mixing, cotangent, preferred_element_type=jnp.float32
    ).astype(jnp.bfloat16)
    feature_grad = feature_grad.reshape(channels, kernels, rows, width)
    spread = adjoint(feature_grad, filter_basis, offsets, counts)
    from_next = passed_along(spread[:, :1].astype(jnp.bfloat16), "lon", -1).astype(jnp.float32)
    from_prev = passed_along(spread[:, -1:].astype(jnp.bfloat16), "lon", 1).astype(jnp.float32)
    inner = spread[:, 1:-1]
    inner = inner.at[:, -1:].add(from_next)
    inner = inner.at[:, :1].add(from_prev)
    banded_grad = (cotangent.astype(jnp.float32) + inner).astype(jnp.bfloat16)
    field_grad = lax.all_to_all(banded_grad, "lon", split_axis=0, concat_axis=1, tiled=True)
    return (mixed_out, field_grad, mixing_grad)


def solution(mesh):
    in_specs = (
        P(("grp", "lon"), None, None),
        P("lon", None, None, None, None),
        P("lon", None),
        P("lon"),
        P(),
        P("grp", "lon", None),
    )
    out_specs = (P("grp", "lon", None), P(("grp", "lon"), None, None), P(("grp", "lon"), None))
    return jax.shard_map(local, mesh=mesh, in_specs=in_specs, out_specs=out_specs, check_vma=False)
```

profile of v0, /device:TPU:28, one launch (start us, length us, event | category | flops | bytes accessed | tf_op | source)
XLA Modules:
  0.0 448.7 jit_solution(3257762338024982644)
XLA Ops:
  10.7 6.0 %all-to-all-start = ((bf16[32,16,1440]{2,0,1:T(8,128)(2,1)}), bf16[32,16,1440]{2,0,1:T(8,128)(2,1)S(1)}, u32[]{:S(2)}, u32[]{:S(2)}) async-start(bf16[32,16,1440]{2,0,1:T(8,128)(2,1)} %copy.64), calls=%async_computation | async-start | bytes 3145728 | tf_op jit(solution)/shard_map/all_to_all | solution.py:118
  16.8 5.9 %convolution_convert_fusion = bf16[1536,1440]{0,1:T(8,128)(2,1)} fusion(bf16[512,1536]{1,0:T(8,128)(2,1)S(1)} %copy-done, bf16[512,1,1440]{0,2,1:T(8,128)(2,1)} %param.23), kind=kOutput, calls=%fused_computation.16 | convolution fusion | flops 2267136000 | bytes 7471104 | tf_op jit(solution)/shard_map/om,orp->mrp/dot_general | solution.py:133
  22.7 6.6 %copy.73 = bf16[1536,1440]{1,0:T(8,128)(2,1)} copy(bf16[1536,1440]{0,1:T(8,128)(2,1)} %convolution_convert_fusion) | data formatting | bytes 8847360 | tf_op jit(solution)/shard_map/convert_element_type | solution.py:135
  29.3 23.2 %reshape_reshape.3 = bf16[512,3,1,45,32]{4,3,1,0,2:T(8,128)(2,1)} reshape(bf16[1536,1440]{1,0:T(8,128)(2,1)} %copy.73) | data formatting | bytes 8847360 | tf_op jit(solution)/shard_map/reshape;reshape | solution.py:78
  52.5 19.5 %copy.74 = bf16[1,45,512,3,32]{2,4,3,1,0:T(8,128)(2,1)} copy(bf16[1,45,512,3,32]{4,1,3,2,0:T(8,128)(2,1)} %bitcast.97) | data formatting | bytes 8847360 | tf_op jit(solution)/shard_map/transpose | solution.py:79
  71.9 4.6 %broadcast.83.clone.1 = f32[45,512,96]{1,2,0:T(8,128)} broadcast(f32[]{:T(128)} %constant.183.clone.1), dimensions={} | broadcast | bytes 8847364 | tf_op jit(solution)/shard_map/broadcast.19
  76.5 69.1 %while.43 = (s32[]{:T(128)}, f32[45,512,96]{1,2,0:T(8,128)}, s32[]{:T(128)}, bf16[6,96,96]{2,1,0:T(8,128)(2,1)S(1)}, bf16[45,512,96]{1,2,0:T(8,128)(2,1)}, /*ind...) while((s32[]{:T(128)}, f32[45,512,96]{1,2,0:T(8,128)}, ...), condition=%wide.region_3.4_spmd, body=%wide.region_2.3_spmd.sunk | while | flops 429096960 | bytes 39837968 | solution.py:97
  82.0 8.2 %fusion.39 = f32[45,512,96]{1,2,0:T(8,128)} fusion(f32[45,512,96]{1,2,0:T(8,128)} %get-tuple-element.447, s32[]{:T(128)S(6)} %select_n.74, f32[45,512,96]{1,2,0:T(8,128)S(1)} %convolution_bitcast_fusion.4), kind=kLoop, calls=%fused_computation.9.clone.1 | loop fusion | flops 4423680 | bytes 26542084 | tf_op jit(solution)/shard_map/while/body/eval_jaxpr/while/body/add | solution.py:95
  95.7 8.2 %fusion.39 = f32[45,512,96]{1,2,0:T(8,128)} fusion(f32[45,512,96]{1,2,0:T(8,128)} %get-tuple-element.447, s32[]{:T(128)S(6)} %select_n.74, f32[45,512,96]{1,2,0:T(8,128)S(1)} %convolution_bitcast_fusion.4), kind=kLoop, calls=%fused_computation.9.clone.1 | loop fusion | flops 4423680 | bytes 26542084 | tf_op jit(solution)/shard_map/while/body/eval_jaxpr/while/body/add | solution.py:95
  109.4 8.2 %fusion.39 = f32[45,512,96]{1,2,0:T(8,128)} fusion(f32[45,512,96]{1,2,0:T(8,128)} %get-tuple-element.447, s32[]{:T(128)S(6)} %select_n.74, f32[45,512,96]{1,2,0:T(8,128)S(1)} %convolution_bitcast_fusion.4), kind=kLoop, calls=%fused_computation.9.clone.1 | loop fusion | flops 4423680 | bytes 26542084 | tf_op jit(solution)/shard_map/while/body/eval_jaxpr/while/body/add | solution.py:95
  123.1 8.2 %fusion.39 = f32[45,512,96]{1,2,0:T(8,128)} fusion(f32[45,512,96]{1,2,0:T(8,128)} %get-tuple-element.447, s32[]{:T(128)S(6)} %select_n.74, f32[45,512,96]{1,2,0:T(8,128)S(1)} %convolution_bitcast_fusion.4), kind=kLoop, calls=%fused_computation.9.clone.1 | loop fusion | flops 4423680 | bytes 26542084 | tf_op jit(solution)/shard_map/while/body/eval_jaxpr/while/body/add | solution.py:95
  136.7 8.2 %fusion.39 = f32[45,512,96]{1,2,0:T(8,128)} fusion(f32[45,512,96]{1,2,0:T(8,128)} %get-tuple-element.447, s32[]{:T(128)S(6)} %select_n.74, f32[45,512,96]{1,2,0:T(8,128)S(1)} %convolution_bitcast_fusion.4), kind=kLoop, calls=%fused_computation.9.clone.1 | loop fusion | flops 4423680 | bytes 26542084 | tf_op jit(solution)/shard_map/while/body/eval_jaxpr/while/body/add | solution.py:95
  158.4 15.9 %collective-permute-start = (bf16[512,1,1440]{0,2,1:T(8,128)(2,1)}, bf16[512,1,1440]{0,2,1:T(8,128)(2,1)}, u32[]{:S(2)}, u32[]{:S(2)}) collective-permute-start(bf16[512,1,1440]{0,2,1:T(8,128)(2,1)} %copy.65), channel_id=1, source_target_pairs={{0,1},{1,2},{2,3},{3,4},{4,5},{5,6},{6,7},{7,8},{8,9},{9,10},{10,1... | collective-permute-start | bytes 4423688 | tf_op jit(solution)/shard_map/ppermute | solution.py:12
  190.5 6.8 %reshape.137 = bf16[512,1,45,32]{3,2,0,1:T(8,128)(2,1)} reshape(bf16[16,32,1,1440]{3,1,0,2:T(8,128)(2,1)S(1)} %bitcast.102) | data formatting | bytes 2949120 | tf_op jit(solution)/shard_map/concatenate | solution.py:16
  197.3 7.3 %copy.81 = bf16[512,1,45,32]{0,3,2,1:T(8,128)(2,1)} copy(bf16[512,1,45,32]{3,2,0,1:T(8,128)(2,1)} %reshape.137) | data formatting | bytes 2949120 | tf_op jit(solution)/shard_map/concatenate | solution.py:16
  209.6 7.8 %pad_maximum_fusion = bf16[90,512,96]{1,2,0:T(8,128)(2,1)} fusion(bf16[45,512,96]{1,2,0:T(8,128)(2,1)} %bitcast.103), kind=kLoop, calls=%fused_computation.14 | loop fusion | flops 4423680 | bytes 13271040 | tf_op jit(solution)/shard_map/while/body/eval_jaxpr/while/body/jit(_roll_dynamic)/concatenate | solution.py:52
  217.4 4.6 %broadcast.83.clone = f32[45,512,96]{1,2,0:T(8,128)} broadcast(f32[]{:T(128)} %constant.183.clone.1), dimensions={} | broadcast | bytes 8847364 | tf_op jit(solution)/shard_map/broadcast.19
  222.0 58.8 %while.42 = (s32[]{:T(128)}, f32[45,512,96]{1,2,0:T(8,128)}, s32[]{:T(128)}, s32[6]{0:T(128)S(1)}, bf16[90,512,96]{1,2,0:T(8,128)(2,1)}, /*index=5*/bf16[6,96,96...) while((s32[]{:T(128)}, f32[45,512,96]{1,2,0:T(8,128)}, ...), condition=%wide.region_1.2_spmd, body=%wide.region_0.1_spmd.sunk | while | flops 426885120 | bytes 22143260 | solution.py:59
  223.9 9.7 %fusion.36 = f32[45,512,96]{1,2,0:T(8,128)} fusion(f32[45,512,96]{1,2,0:T(8,128)} %get-tuple-element.411, bf16[90,512,96]{1,2,0:T(8,128)(2,1)} %get-tuple-element.426, s32[]{:T(128)S(6)} %select_n.71, bf16[6,96,96]{2,1,0:T(8,128)(2,1)S(1)} %get-tuple-element.427, s32[]{:T(128)S(6)} %select_n.69), kind=kOutput, calls=%fused_computation.2.clone.1 | convolution fusion | flops 426885120 | bytes 22142984 | tf_op jit(solution)/shard_map/while/body/eval_jaxpr/while/body/bcx,xy->bcy/dot_general | solution.py:53
  235.5 9.7 %fusion.36 = f32[45,512,96]{1,2,0:T(8,128)} fusion(f32[45,512,96]{1,2,0:T(8,128)} %get-tuple-element.411, bf16[90,512,96]{1,2,0:T(8,128)(2,1)} %get-tuple-element.426, s32[]{:T(128)S(6)} %select_n.71, bf16[6,96,96]{2,1,0:T(8,128)(2,1)S(1)} %get-tuple-element.427, s32[]{:T(128)S(6)} %select_n.69), kind=kOutput, calls=%fused_computation.2.clone.1 | convolution fusion | flops 426885120 | bytes 22142984 | tf_op jit(solution)/shard_map/while/body/eval_jaxpr/while/body/bcx,xy->bcy/dot_general | solution.py:53
  247.0 9.6 %fusion.36 = f32[45,512,96]{1,2,0:T(8,128)} fusion(f32[45,512,96]{1,2,0:T(8,128)} %get-tuple-element.411, bf16[90,512,96]{1,2,0:T(8,128)(2,1)} %get-tuple-element.426, s32[]{:T(128)S(6)} %select_n.71, bf16[6,96,96]{2,1,0:T(8,128)(2,1)S(1)} %get-tuple-element.427, s32[]{:T(128)S(6)} %select_n.69), kind=kOutput, calls=%fused_computation.2.clone.1 | convolution fusion | flops 426885120 | bytes 22142984 | tf_op jit(solution)/shard_map/while/body/eval_jaxpr/while/body/bcx,xy->bcy/dot_general | solution.py:53
  258.6 9.7 %fusion.36 = f32[45,512,96]{1,2,0:T(8,128)} fusion(f32[45,512,96]{1,2,0:T(8,128)} %get-tuple-element.411, bf16[90,512,96]{1,2,0:T(8,128)(2,1)} %get-tuple-element.426, s32[]{:T(128)S(6)} %select_n.71, bf16[6,96,96]{2,1,0:T(8,128)(2,1)S(1)} %get-tuple-element.427, s32[]{:T(128)S(6)} %select_n.69), kind=kOutput, calls=%fused_computation.2.clone.1 | convolution fusion | flops 426885120 | bytes 22142984 | tf_op jit(solution)/shard_map/while/body/eval_jaxpr/while/body/bcx,xy->bcy/dot_general | solution.py:53
  270.2 9.7 %fusion.36 = f32[45,512,96]{1,2,0:T(8,128)} fusion(f32[45,512,96]{1,2,0:T(8,128)} %get-tuple-element.411, bf16[90,512,96]{1,2,0:T(8,128)(2,1)} %get-tuple-element.426, s32[]{:T(128)S(6)} %select_n.71, bf16[6,96,96]{2,1,0:T(8,128)(2,1)S(1)} %get-tuple-element.427, s32[]{:T(128)S(6)} %select_n.69), kind=kOutput, calls=%fused_computation.2.clone.1 | convolution fusion | flops 426885120 | bytes 22142984 | tf_op jit(solution)/shard_map/while/body/eval_jaxpr/while/body/bcx,xy->bcy/dot_general | solution.py:53
  280.7 6.3 %convert_element_type.59 = bf16[45,512,96]{1,2,0:T(8,128)(2,1)} convert(f32[45,512,96]{1,2,0:T(8,128)} %get-tuple-element.245) | non-fusion elementwise | flops 2211840 | bytes 13271040 | tf_op jit(solution)/shard_map/convert_element_type | solution.py:120
  287.0 21.0 %copy.71 = bf16[1,45,512,3,32]{4,1,3,2,0:T(8,128)(2,1)} copy(bf16[1,45,512,3,32]{2,4,3,1,0:T(8,128)(2,1)} %bitcast.104) | data formatting | bytes 8847360 | tf_op jit(solution)/shard_map/convert_element_type | solution.py:120
  308.1 24.2 %convert_element_type.62 = bf16[1536,1440]{1,0:T(8,128)(2,1)} reshape(bf16[512,3,1,45,32]{4,3,1,0,2:T(8,128)(2,1)} %bitcast.98) | data formatting | bytes 8847360 | tf_op jit(solution)/shard_map/convert_element_type | solution.py:120
  332.2 7.1 %convolution_bitcast_fusion.1 = f32[512,1536]{0,1:T(8,128)} fusion(bf16[1536,1440]{1,0:T(8,128)(2,1)} %convert_element_type.62, bf16[512,1,1440]{0,2,1:T(8,128)(2,1)} %param.23), kind=kOutput, calls=%fused_computation.18 | convolution fusion | flops 2264924160 | bytes 9043968 | tf_op jit(solution)/shard_map/orp,mrp->om/dot_general | solution.py:128
  342.9 5.1 %fusion.17 = bf16[512,1,1440]{0,2,1:T(8,128)(2,1)} fusion(f32[512,3,1440]{0,2,1:T(8,128)} %get-tuple-element.317, bf16[512,1,1440]{0,2,1:T(8,128)(2,1)} %collective-permute-done.3, bf16[512,1,1440]{0,2,1:T(8,128)(2,1)} %collective-permute-done.2, bf16[512,1,1440]{0,2,1:T(8,128)(2,1)} %param.23), kind=kLoop, calls=%fused_computation.25 | loop fusion | flops 5160960 | bytes 8847360 | tf_op jit(solution)/shard_map/convert_element_type | solution.py:143
  354.8 5.5 %reshape.140 = bf16[16,2,23040]{2,1,0:T(2,128)(2,1)} reshape(bf16[512,1440]{1,0:T(8,128)(2,1)} %copy.86) | data formatting | bytes 2949120
  360.3 17.1 %all-to-all-start.1 = ((bf16[16,2,23040]{2,1,0:T(2,128)(2,1)}), bf16[16,2,23040]{2,1,0:T(2,128)(2,1)}, u32[]{:S(2)}, u32[]{:S(2)}) async-start(bf16[16,2,23040]{2,1,0:T(2,128)(2,1)} %reshape.140), calls=%async_computation.1 | async-start | bytes 2949120 | tf_op jit(solution)/shard_map/all_to_all | solution.py:144
  383.1 39.9 %all-to-all-done.1 = bf16[16,2,23040]{2,1,0:T(2,128)(2,1)} async-done(((bf16[16,2,23040]{2,1,0:T(2,128)(2,1)}), bf16[16,2,23040]{2,1,0:T(2,128)(2,1)}, u32[]{:S(2)}, u32[]{:S(2)}) %all-to-all-start.1) | async-done | bytes 1474592 | tf_op jit(solution)/shard_map/all_to_all | solution.py:144
  423.0 10.5 %reshape.141 = bf16[512,1,1440]{2,1,0:T(2,128)(2,1)} reshape(bf16[16,2,23040]{2,1,0:T(2,128)(2,1)} %all-to-all-done.1) | data formatting | bytes 2949120
  (64 shorter events, 85.7 us)
Async XLA Ops:
  7.2 9.7 %copy-start = (bf16[512,1536]{1,0:T(8,128)(2,1)S(1)}, bf16[512,1536]{1,0:T(8,128)(2,1)}, u32[]{:S(2)}) copy-start(bf16[512,1536]{1,0:T(8,128)(2,1)} %param.22) | copy-start | bytes 4718596
  7.2 9.6 %copy-start.5 = (bf16[1,3,6,32,96]{4,3,2,1,0:T(8,128)(2,1)S(1)}, bf16[1,3,6,32,96]{4,3,2,1,0:T(8,128)(2,1)}, u32[]{:S(2)}) copy-start(bf16[1,3,6,32,96]{4,3,2,1,0:T(8,128)(2,1)} %param.19) | copy-start | bytes 331780
  10.7 146.1 %all-to-all-start = ((bf16[32,16,1440]{2,0,1:T(8,128)(2,1)}), bf16[32,16,1440]{2,0,1:T(8,128)(2,1)S(1)}, u32[]{:S(2)}, u32[]{:S(2)}) async-start(bf16[32,16,1440]{2,0,1:T(8,128)(2,1)} %copy.64), calls=%async_computation | async-start | bytes 3145728 | tf_op jit(solution)/shard_map/all_to_all | solution.py:118
  16.8 425.1 %reduce-scatter.4.cloned.1.call-start = ((), (), s32[]{:S(2)}) async-start(), calls=%async_computation.3 | async-start | bytes 3342336
  71.9 4.6 %copy-start.6 = (s32[1,6]{1,0:T(1,128)S(1)}, s32[1,6]{1,0:T(1,128)}, u32[]{:S(2)}) copy-start(s32[1,6]{1,0:T(1,128)} %param.20) | copy-start | bytes 76
  150.1 3.4 copy-start.1
  158.4 20.2 %copy-start.2 = (f32[512,1,1440]{0,2,1:T(8,128)S(1)}, f32[512,1,1440]{0,2,1:T(8,128)}, u32[]{:S(2)}) copy-start(f32[512,1,1440]{0,2,1:T(8,128)} %get-tuple-element.318) | copy-start | bytes 8847364
  158.4 20.2 %copy-start.3 = (f32[512,1,1440]{0,2,1:T(8,128)S(1)}, f32[512,1,1440]{0,2,1:T(8,128)}, u32[]{:S(2)}) copy-start(f32[512,1,1440]{0,2,1:T(8,128)} %get-tuple-element.319) | copy-start | bytes 8847364
  158.4 46.2 %collective-permute-start = (bf16[512,1,1440]{0,2,1:T(8,128)(2,1)}, bf16[512,1,1440]{0,2,1:T(8,128)(2,1)}, u32[]{:S(2)}, u32[]{:S(2)}) collective-permute-start(bf16[512,1,1440]{0,2,1:T(8,128)(2,1)} %copy.65), channel_id=1, source_target_pairs={{0,1},{1,2},{2,3},{3,4},{4,5},{5,6},{6,7},{7,8},{8,9},{9,10},{10,1... | collective-permute-start | bytes 4423688 | tf_op jit(solution)/shard_map/ppermute | solution.py:12
  174.3 30.3 %collective-permute-start.1 = (bf16[512,1,1440]{0,2,1:T(8,128)(2,1)}, bf16[512,1,1440]{0,2,1:T(8,128)(2,1)}, u32[]{:S(2)}, u32[]{:S(2)}) collective-permute-start(bf16[512,1,1440]{0,2,1:T(8,128)(2,1)} %copy.65), channel_id=1, source_target_pairs={{1,0},{2,1},{3,2},{4,3},{5,4},{6,5},{7,6},{8,7},{9,8},{10,9},{11,1... | collective-permute-start | bytes 4423688 | tf_op jit(solution)/shard_map/ppermute | solution.py:15
  184.8 158.1 %collective-permute-start.2 = (bf16[512,1,1440]{0,2,1:T(8,128)(2,1)}, bf16[512,1,1440]{0,2,1:T(8,128)(2,1)}, u32[]{:S(2)}, u32[]{:S(2)}) collective-permute-start(bf16[512,1,1440]{0,2,1:T(8,128)(2,1)} %get-tuple-element.320), channel_id=1, source_target_pairs={{1,0},{2,1},{3,2},{4,3},{5,4},{6,5},{7,6},{8,7},{9,8},{10,9},{11,1... | collective-permute-start | bytes 4423688 | tf_op jit(solution)/shard_map/ppermute | solution.py:23
  186.7 156.2 %collective-permute-start.3 = (bf16[512,1,1440]{0,2,1:T(8,128)(2,1)}, bf16[512,1,1440]{0,2,1:T(8,128)(2,1)}, u32[]{:S(2)}, u32[]{:S(2)}) collective-permute-start(bf16[512,1,1440]{0,2,1:T(8,128)(2,1)} %get-tuple-element.321), channel_id=1, source_target_pairs={{0,1},{1,2},{2,3},{3,4},{4,5},{5,6},{6,7},{7,8},{8,9},{9,10},{10,1... | collective-permute-start | bytes 4423688 | tf_op jit(solution)/shard_map/ppermute | solution.py:23
  360.3 62.7 %all-to-all-start.1 = ((bf16[16,2,23040]{2,1,0:T(2,128)(2,1)}), bf16[16,2,23040]{2,1,0:T(2,128)(2,1)}, u32[]{:S(2)}, u32[]{:S(2)}) async-start(bf16[16,2,23040]{2,1,0:T(2,128)(2,1)} %reshape.140), calls=%async_computation.1 | async-start | bytes 2949120 | tf_op jit(solution)/shard_map/all_to_all | solution.py:144
  423.0 15.0 %slice-start = ((s8[4718592]{0:T(1024)(128)(4,1)}), s8[524288]{0:T(1024)(128)(4,1)S(1)}, s32[]{:S(2)}) async-start(s8[4718592]{0:T(1024)(128)(4,1)} %bitcast.106), calls=%async_computation.4 | async-start | bytes 1048576
  433.6 4.4 slice-start.1
  433.6 4.4 copy-start.4
Sparse Core Ops, SparseCore 0:
  343.0 93.2 reduce-scatter.3
where the time goes:
time: 455 us; the launch traced here: 449 us
  local copies, waits for them, and re-layouts  177 us (39%)
  matrix products  82.9 us (18%)
  other arithmetic  73 us (16%)
  starting transfers between devices  46.9 us (10%)
  waiting for transfers between devices  39.9 us (9%)
  loops' own time  14.9 us (3%)
  between operations  14.2 us (3%)
    dot_general x5, matrix products, contract_slot_term(): jnp.einsum('bcx,xy->bcy', shifted, piece, preferred_element_type=jnp.floa...  48.3 us
    convert_element_type x2, local copies, waits for them, and re-layouts, local(): contract(extended, filter_basis, offsets, counts).astype(jnp.bfloat16)  45.2 us
    add x5, other arithmetic, adjoint_add_slot(): return total + adjoint_slot_term(slot, piece)  41 us
    all_to_all x1, waiting for transfers between devices, local(): lax.all_to_all(banded_grad, 'lon', split_axis=0, concat_axis=1, tiled=True)  39.9 us
    unnamed x25, local copies, waits for them, and re-layouts  33.5 us
    another operation x1, local copies, waits for them, and re-layouts, adjoint(): grads.reshape(channels, kernels, rows, nblocks, block)  23.2 us
    transpose x1, local copies, waits for them, and re-layouts, adjoint(): blocked = grads.reshape(channels, kernels, rows, nblocks, block).transpos...  19.5 us
    dot_general x5, matrix products, adjoint_slot_term(): jnp.einsum('bcy,xy->bcx', row, piece, preferred_element_type=jnp.float32)  17.8 us
  transfers between devices with their start and end apart: 7, of which 1 were waited for; matrix products, arithmetic and copies ran while one was open for 72% of the time, Pallas kernels for 0%

commit v1 on v0

v1 whole, which is shorter than its diff:
```python
import functools

import jax
import jax.numpy as jnp
from jax import lax
from jax.experimental import pallas as pl
from jax.experimental.pallas import tpu as pltpu
from jax.sharding import PartitionSpec as P

F32 = jnp.float32
BF16 = jnp.bfloat16


def spread_columns(channels, kernels, dtype):
    size = channels * kernels
    row = lax.broadcasted_iota(jnp.int32, (size, size), 0)
    col = lax.broadcasted_iota(jnp.int32, (size, size), 1)
    return ((row % channels) * kernels + row // channels == col).astype(dtype)


def adjoint_kernel(kernels, block, slots, off_ref, cot_ref, mix_ref, w_ref, a0_ref, a1_ref, a2_ref, g_ref):
    width, channels = cot_ref.shape
    nblocks = width // block
    rows = block * 9

    @pl.loop(0, width // rows)
    def _(step):
        at = pl.ds(pl.multiple_of(step * rows, rows), rows)
        for k in range(kernels):
            g_ref[at, k * channels:(k + 1) * channels] = jnp.dot(
                cot_ref[at, :], mix_ref[:, k * channels:(k + 1) * channels], preferred_element_type=F32
            ).astype(BF16)

    @pl.loop(0, nblocks)
    def _(b):
        parts = []
        for s in range(slots):
            src = b - off_ref[0, s]
            src = jnp.where(src < 0, src + nblocks, src)
            at = pl.ds(pl.multiple_of(src * block, block), block)
            for k in range(kernels):
                parts.append(g_ref[at, k * channels:(k + 1) * channels])
        out = jnp.dot(w_ref[...], jnp.concatenate(parts, axis=0), preferred_element_type=F32)
        at = pl.ds(pl.multiple_of(b * block, block), block)
        a0_ref[at, :] = out[:block].astype(BF16)
        a1_ref[at, :] = out[block:2 * block] + cot_ref[at, :].astype(F32)
        a2_ref[at, :] = out[2 * block:].astype(BF16)


def forward_kernel(kernels, block, slots, off_ref, x0_ref, x1_ref, x2_ref, cot_ref, mix_ref, w_ref,
                   out_ref, grad_ref, f_ref):
    width, channels = x1_ref.shape
    nblocks = width // block
    rows = block * 9

    @pl.loop(0, nblocks)
    def _(b):
        parts = []
        for s in range(slots):
            src = b + off_ref[0, s]
            src = jnp.where(src >= nblocks, src - nblocks, src)
            at = pl.ds(pl.multiple_of(src * block, block), block)
            for x_ref in (x0_ref, x1_ref, x2_ref):
                parts.append(x_ref[at, :])
        out = jnp.dot(w_ref[...], jnp.concatenate(parts, axis=0), preferred_element_type=F32).astype(BF16)
        at = pl.ds(pl.multiple_of(b * block, block), block)
        for k in range(kernels):
            f_ref[at, k * channels:(k + 1) * channels] = out[k * block:(k + 1) * block]

    @pl.loop(0, width // rows)
    def _(step):
        at = pl.ds(pl.multiple_of(step * rows, rows), rows)
        mixed = lax.dot_general(
            f_ref[at, :], mix_ref[...], (((1,), (1,)), ((), ())), preferred_element_type=F32
        )
        out_ref[at, :] = (x1_ref[at, :].astype(F32) + mixed).astype(BF16)

    for k in range(kernels):
        grad_ref[:, k * channels:(k + 1) * channels] = jnp.dot(
            cot_ref[...], f_ref[:, k * channels:(k + 1) * channels], preferred_element_type=F32
        ).astype(grad_ref.dtype)


def passed_along(value, axis, steps):
    count = lax.axis_size(axis)
    leading, last = (max(0, -steps), min(count, count - steps))
    return lax.ppermute(value, axis, [(source, source + steps) for source in range(leading, last)])


def local(fields, filter_basis, offsets, counts, mixing, cotangent):
    channels, cols = mixing.shape
    kernels = cols // channels
    _, taps, slots, block, outer = filter_basis.shape
    width = fields.shape[2]
    vmem = pl.BlockSpec(memory_space=pltpu.VMEM)
    smem = pl.BlockSpec(memory_space=pltpu.SMEM)
    params = pltpu.CompilerParams(vmem_limit_bytes=48 * 2**20)

    own = lax.all_to_all(fields.transpose(1, 0, 2), "lon", split_axis=0, concat_axis=0, tiled=True)
    own = own.reshape(channels, width)

    live = jnp.arange(slots) < counts[0]
    basis = jnp.where(live[None, :, None, None], filter_basis[0], 0)
    w_adj = basis.transpose(0, 2, 1, 3).reshape(taps * block, slots * outer)
    w_fwd = basis.transpose(3, 1, 0, 2).reshape(outer, slots * taps * block)
    perm = spread_columns(channels, kernels, BF16)
    mix = lax.dot_general(mixing, perm, (((1,), (1,)), ((), ())), preferred_element_type=F32).astype(BF16)
    cot = cotangent[:, 0, :]
    cot_t = cot.T

    a0, a1, a2 = pl.pallas_call(
        functools.partial(adjoint_kernel, kernels, block, slots),
        out_shape=[
            jax.ShapeDtypeStruct((width, channels), BF16),
            jax.ShapeDtypeStruct((width, channels), F32),
            jax.ShapeDtypeStruct((width, channels), BF16),
        ],
        in_specs=[smem, vmem, vmem, vmem],
        out_specs=[vmem] * 3,
        scratch_shapes=[pltpu.VMEM((width, cols), BF16)],
        compiler_params=params,
        cost_estimate=pl.CostEstimate(flops=3 * 10**10, bytes_accessed=10**7, transcendentals=0),
        name="adjoint",
    )(offsets, cot_t, mix, w_adj)
    from_next = passed_along(a0, "lon", -1)
    from_prev = passed_along(a2, "lon", 1)

    own_t = own.T
    below = passed_along(own_t, "lon", 1)
    above = passed_along(own_t, "lon", -1)

    banded = (a1 + from_next.astype(F32) + from_prev.astype(F32)).astype(BF16).T
    banded = banded.reshape(lax.axis_size("lon"), -1, width)
    field_grad = lax.all_to_all(banded, "lon", split_axis=0, concat_axis=0, tiled=True).transpose(1, 0, 2)

    mixed_t, grad = pl.pallas_call(
        functools.partial(forward_kernel, kernels, block, slots),
        out_shape=[
            jax.ShapeDtypeStruct((width, channels), BF16),
            jax.ShapeDtypeStruct((channels, cols), F32),
        ],
        in_specs=[smem] + [vmem] * 6,
        out_specs=[vmem] * 2,
        scratch_shapes=[pltpu.VMEM((width, cols), BF16)],
        compiler_params=params,
        cost_estimate=pl.CostEstimate(flops=3 * 10**10, bytes_accessed=10**7, transcendentals=0),
        name="forward",
    )(offsets, below, own_t, above, cot, mix, w_fwd)
    grad = lax.psum_scatter(grad, "lon", scatter_dimension=0, tiled=True)
    grad = lax.dot(grad, spread_columns(channels, kernels, F32), precision=lax.Precision.HIGHEST)
    return mixed_t.T[:, None, :], field_grad, grad


def solution(mesh):
    in_specs = (
        P(("grp", "lon"), None, None),
        P("lon", None, None, None, None),
        P("lon", None),
        P("lon"),
        P(),
        P("grp", "lon", None),
    )
    out_specs = (P("grp", "lon", None), P(("grp", "lon"), None, None), P(("grp", "lon"), None))
    return jax.shard_map(local, mesh=mesh, in_specs=in_specs, out_specs=out_specs, check_vma=False)
```

time: 455 us -> 221 us (0.49)
  local copies, waits for them, and re-layouts: 177 us -> 14.7 us
  matrix products: 82.9 us -> 11.3 us
  other arithmetic: 73 us -> 4.54 us
  blocking collectives: 0 us -> 56 us
  Pallas kernels: 0 us -> 39.2 us
  starting transfers between devices: 46.9 us -> 17 us
  waiting for transfers between devices: 39.9 us -> 59.3 us
  loops' own time: 14.9 us -> 0 us
    dot_general x13 -> x2, matrix products: 82.9 us -> 11.3 us  [the longest x1 5.91 us: local(): lax.dot_general(mixing, perm, (((1,), (1,)), ((), ())), preferred_element...]
    all_to_all x0 -> x1, blocking collectives: none -> 56 us  [local(): lax.all_to_all(banded, 'lon', split_axis=0, concat_axis=0, tiled=True)]
    convert_element_type x5 -> x0, local copies, waits for them, and re-layouts: 55.8 us -> none  [the longest x2 45.2 us: local(): contract(extended, filter_basis, offsets, counts).astype(jnp.bfloat16)]
    add x5 -> x1, other arithmetic: 41 us -> 0.01 us  [spread_columns(): return (row % channels * kernels + row // channels == col).astype(dtype)]
    pallas_call x0 -> x2, Pallas kernels: none -> 39.2 us  [the longest x1 21.5 us: local(): pl.pallas_call(functools.partial(forward_kernel, kernels, block, slots),...]
    another operation x3 -> x0, local copies, waits for them, and re-layouts: 32.3 us -> none  [the longest x1 23.2 us: adjoint(): grads.reshape(channels, kernels, rows, nblocks, block)]
    unnamed x25 -> x14, local copies, waits for them, and re-layouts: 33.5 us -> 8.34 us
    transpose x4 -> x3, local copies, waits for them, and re-layouts: 26.5 us -> 1.77 us  [the longest x1 1.69 us: local(): banded = (a1 + from_next.astype(F32) + from_prev.astype(F32)).astype(BF16).T]
  transfers between devices with their start and end apart: 7 -> 6, of which waited for: 1 -> 3; matrix products, arithmetic and copies ran while one was open for 72% -> 7% of each run, Pallas kernels for 0% -> 18%
where the time goes in v1:
time: 221 us; the launch traced here: 217 us
  waiting for transfers between devices  59.3 us (27%)
  blocking collectives  56 us (25%)
  Pallas kernels  39.2 us (18%)
  starting transfers between devices  17 us (8%)
  between operations  14.8 us (7%)
  local copies, waits for them, and re-layouts  14.7 us (7%)
  matrix products  11.3 us (5%)
  other arithmetic  4.54 us (2%)
    all_to_all x1, blocking collectives, local(): lax.all_to_all(banded, 'lon', split_axis=0, concat_axis=0, tiled=True)  56 us
    all_to_all x1, waiting for transfers between devices, local(): lax.all_to_all(fields.transpose(1, 0, 2), 'lon', split_axis=0, concat_axi...  28.2 us
    pallas_call x1, Pallas kernels, local(): pl.pallas_call(functools.partial(forward_kernel, kernels, block, slots),...  21.5 us
    ppermute x4, waiting for transfers between devices, passed_along(): lax.ppermute(value, axis, [(source, source + steps) for source in range(l...  18.9 us
    pallas_call x1, Pallas kernels, local(): pl.pallas_call(functools.partial(adjoint_kernel, kernels, block, slots),...  17.7 us
    reduce_scatter x1, waiting for transfers between devices, local(): grad = lax.psum_scatter(grad, 'lon', scatter_dimension=0, tiled=True)  12.2 us
    ppermute x4, starting transfers between devices, passed_along(): lax.ppermute(value, axis, [(source, source + steps) for source in range(l...  10.8 us
    unnamed x14, local copies, waits for them, and re-layouts  8.34 us
  transfers between devices with their start and end apart: 6, of which 3 were waited for; matrix products, arithmetic and copies ran while one was open for 7% of the time, Pallas kernels for 18%

profile of v1, /device:TPU:28, one launch (start us, length us, event | category | flops | bytes accessed | tf_op | source)
XLA Modules:
  0.0 216.8 jit_solution(17203715440190154917)
XLA Ops:
  7.2 0.0 copy-start
  7.2 3.5 %copy.35 = bf16[32,16,1440]{2,0,1:T(8,128)(2,1)} copy(bf16[32,16,1440]{2,1,0:T(8,128)(2,1)} %param.6) | data formatting | bytes 2949120 | tf_op args[0]
  10.7 6.1 %all-to-all-start = ((bf16[16,32,1440]{2,1,0:T(8,128)(2,1)}), bf16[16,32,1440]{2,1,0:T(8,128)(2,1)}, u32[]{:S(2)}, u32[]{:S(2)}) async-start(bf16[16,32,1440]{2,1,0:T(8,128)(2,1)} %bitcast.30), calls=%async_computation | async-start | bytes 3145728 | tf_op jit(solution)/shard_map/all_to_all | solution.py:99
  16.9 0.0 reduce-scatter.2.cloned.1.call-start
  17.6 0.0 copy-done.5
  17.6 0.1 fusion.2
  17.7 0.1 copy.30
  17.8 0.1 reshape.24.w_ref
  17.9 5.9 %fusion.mix_ref = bf16[512,1536]{1,0:T(8,128)(2,1)} fusion(bf16[512,1536]{1,0:T(8,128)(2,1)S(1)} %copy-done, s32[1536]{0:T(1024)S(1)} %get-tuple-element.21, s32[1536]{0:T(1024)S(1)} %get-tuple-element.24, s32[1536]{0:T(1024)S(1)} %get-tuple-element.22, s32[1536]{0:T(1024)S(1)} %get-tuple-element.23, pred[1536]{0:T(1024)(128)(4,1)S(1)} %get-tuple-element.25, ...), kind=kOutput, calls=%fused_computation.3 | convolution fusion | flops 2428502016 | bytes 3173376 | tf_op jit(solution)/shard_map/dot_general | solution.py:107
  23.9 28.2 %all-to-all-done = bf16[16,32,1440]{2,1,0:T(8,128)(2,1)} async-done(((bf16[16,32,1440]{2,1,0:T(8,128)(2,1)}), bf16[16,32,1440]{2,1,0:T(8,128)(2,1)}, u32[]{:S(2)}, u32[]{:S(2)}) %all-to-all-start) | async-done | bytes 1474592 | tf_op jit(solution)/shard_map/all_to_all | solution.py:99
  52.0 2.6 %copy.25 = bf16[512,1440]{0,1:T(8,128)(2,1)} copy(bf16[512,1440]{1,0:T(8,128)(2,1)} %bitcast.1) | data formatting | bytes 2949120 | tf_op jit(solution)/shard_map/reshape | solution.py:100
  54.6 1.9 collective-permute-start.1
  56.5 3.5 %collective-permute-start = (bf16[1440,512]{1,0:T(8,128)(2,1)}, bf16[1440,512]{1,0:T(8,128)(2,1)}, u32[]{:S(2)}, u32[]{:S(2)}) collective-permute-start(bf16[1440,512]{1,0:T(8,128)(2,1)} %bitcast.35), channel_id=1, source_target_pairs={{0,1},{1,2},{2,3},{3,4},{4,5},{5,6},{6,7},{7,8},{8,9},{9,10},{10,1... | collective-permute-start | bytes 4423688 | tf_op jit(solution)/shard_map/ppermute | solution.py:87
  60.1 1.4 copy-done.4
  61.5 17.7 %adjoint.1 = (bf16[1440,512]{1,0:T(8,128)(2,1)}, f32[1440,512]{1,0:T(8,128)}, bf16[1440,512]{1,0:T(8,128)(2,1)}) custom-call(s32[1,6]{1,0:T(1,128)S(1)} %copy-done.3, bf16[1440,512]{1,0:T(8,128)(2,1)S(1)} %bitcast.33, bf16[512,1536]{1,0:T(8,128)(2,1)S(1)} %copy-done.4, bf16[96,576]{1,0:T(8,128)(2,1)S(1)} %reshape.24.w_ref), custom_call_target="tpu_custom_call" | custom-call | flops 30000001024 | bytes 10000000 | tf_op jit(solution)/shard_map/adjoint/pallas_call | solution.py:111
  79.1 2.0 collective-permute-start.2
  81.2 3.4 %collective-permute-start.3 = (bf16[1440,512]{1,0:T(8,128)(2,1)}, bf16[1440,512]{1,0:T(8,128)(2,1)}, u32[]{:S(2)}, u32[]{:S(2)}) collective-permute-start(bf16[1440,512]{1,0:T(8,128)(2,1)} %get-tuple-element.11), channel_id=1, source_target_pairs={{0,1},{1,2},{2,3},{3,4},{4,5},{5,6},{6,7},{7,8},{8,9},{9,10},{10,1... | collective-permute-start | bytes 4423688 | tf_op jit(solution)/shard_map/ppermute | solution.py:87
  84.6 0.2 copy.29.w_ref
  84.7 1.7 copy.28.cot_ref
  86.4 18.9 %collective-permute-done.1.x2_ref = bf16[1440,512]{1,0:T(8,128)(2,1)} collective-permute-done((bf16[1440,512]{1,0:T(8,128)(2,1)}, bf16[1440,512]{1,0:T(8,128)(2,1)}, u32[]{:S(2)}, u32[]{:S(2)}) %collective-permute-start.1) | collective-permute-done | bytes 1474592 | tf_op jit(solution)/shard_map/ppermute | solution.py:87
  105.3 0.0 collective-permute-done.x0_ref
  105.3 1.4 copy-done.2
  106.7 21.5 %forward.1 = (bf16[1440,512]{1,0:T(8,128)(2,1)}, f32[512,1536]{1,0:T(8,128)}) custom-call(s32[1,6]{1,0:T(1,128)S(1)} %copy-done.3, bf16[1440,512]{1,0:T(8,128)(2,1)} %collective-permute-done.x0_ref, bf16[1440,512]{1,0:T(8,128)(2,1)S(1)} %bitcast.36, bf16[1440,512]{1,0:T(8,128)(2,1)} %collective-permute-done.1.x2_ref, bf16[512,1440]{1,0:T(8,128)(2,1)S(1)} %copy.28.cot_ref, ...), custom_call_target="tpu_custom_call" | custom-call | flops 30000001024 | bytes 10000000 | tf_op jit(solution)/shard_map/forward/pallas_call | solution.py:136
  128.2 0.0 reduce-scatter.2.cloned.1.call-update
  128.2 0.0 collective-permute-done.2
  128.2 0.0 collective-permute-done.3
  128.2 4.4 %fusion.1 = bf16[512,1440]{0,1:T(8,128)(2,1)} fusion(bf16[1440,512]{1,0:T(8,128)(2,1)} %collective-permute-done.3, f32[1440,512]{1,0:T(8,128)} %get-tuple-element.9, bf16[1440,512]{1,0:T(8,128)(2,1)} %collective-permute-done.2), kind=kLoop, calls=%fused_computation.5 | loop fusion | flops 3686400 | bytes 7372800 | tf_op jit(solution)/shard_map/transpose | solution.py:132
  132.7 1.7 copy.31
  134.4 56.0 %all_to_all.10 = bf16[16,32,1440]{2,1,0:T(8,128)(2,1)S(1)} all-to-all(bf16[16,32,1440]{2,1,0:T(8,128)(2,1)S(1)} %bitcast.37), channel_id=1, replica_groups=mesh['grp'=2,'lon'=16] {'lon'}, dimensions={0} | all-to-all | bytes 2949120 | tf_op jit(solution)/shard_map/all_to_all | solution.py:134
  190.4 2.0 copy.32
  192.4 12.2 %reduce-scatter.2.cloned.1.call-done = f32[32,1536]{1,0:T(8,128)} async-done(((f32[512,1536]{1,0:T(8,128)}), f32[32,1536]{1,0:T(8,128)}) %reduce-scatter.2.cloned.1.call-update) | async-done | bytes 196624 | tf_op jit(solution)/shard_map/reduce_scatter | solution.py:149
  204.6 5.4 %fusion.10 = f32[32,1536]{1,0:T(8,128)} fusion(f32[32,1536]{1,0:T(8,128)} %reduce-scatter.2.cloned.1.call-done, s32[1536]{0:T(1024)S(1)} %get-tuple-element.21, s32[1536]{0:T(1024)S(1)} %get-tuple-element.24, s32[1536]{0:T(1024)S(1)} %get-tuple-element.22, s32[1536]{0:T(1024)S(1)} %get-tuple-element.23, pred[1536]{0:T(1024)(128)(4,1)S(1)} %get-tuple-element.25, ...), kind=kOutput, calls=%fused_computation.20 | convolution fusion | flops 917766144 | bytes 420864 | tf_op jit(solution)/shard_map/dot_general | solution.py:150
  (13 shorter events, 0.1 us)
Async XLA Ops:
  7.2 10.8 %copy-start = (bf16[512,1536]{1,0:T(8,128)(2,1)S(1)}, bf16[512,1536]{1,0:T(8,128)(2,1)}, u32[]{:S(2)}) copy-start(bf16[512,1536]{1,0:T(8,128)(2,1)} %param.10) | copy-start | bytes 4718596
  10.7 6.9 %copy-start.5 = (bf16[1,3,6,32,96]{4,3,2,1,0:T(8,128)(2,1)S(1)}, bf16[1,3,6,32,96]{4,3,2,1,0:T(8,128)(2,1)}, u32[]{:S(2)}) copy-start(bf16[1,3,6,32,96]{4,3,2,1,0:T(8,128)(2,1)} %param.7) | copy-start | bytes 331780
  10.7 41.3 %all-to-all-start = ((bf16[16,32,1440]{2,1,0:T(8,128)(2,1)}), bf16[16,32,1440]{2,1,0:T(8,128)(2,1)}, u32[]{:S(2)}, u32[]{:S(2)}) async-start(bf16[16,32,1440]{2,1,0:T(8,128)(2,1)} %bitcast.30), calls=%async_computation | async-start | bytes 3145728 | tf_op jit(solution)/shard_map/all_to_all | solution.py:99
  16.9 187.7 %reduce-scatter.2.cloned.1.call-start = ((), (), s32[]{:S(2)}) async-start(), calls=%async_computation.3 | async-start | bytes 3342336 | tf_op jit(solution)/shard_map/reduce_scatter | solution.py:149
  23.9 36.2 %copy-start.1 = (bf16[512,1,1440]{0,2,1:T(8,128)(2,1)S(1)}, bf16[512,1,1440]{0,2,1:T(8,128)(2,1)}, u32[]{:S(2)}) copy-start(bf16[512,1,1440]{0,2,1:T(8,128)(2,1)} %param.11) | copy-start | bytes 4423684
  23.9 36.2 %copy-start.3 = (s32[1,6]{1,0:T(1,128)S(1)}, s32[1,6]{1,0:T(1,128)}, u32[]{:S(2)}) copy-start(s32[1,6]{1,0:T(1,128)} %off_ref.3) | copy-start | bytes 76
  54.6 50.7 %collective-permute-start.1 = (bf16[1440,512]{1,0:T(8,128)(2,1)}, bf16[1440,512]{1,0:T(8,128)(2,1)}, u32[]{:S(2)}, u32[]{:S(2)}) collective-permute-start(bf16[1440,512]{1,0:T(8,128)(2,1)} %bitcast.34), channel_id=1, source_target_pairs={{1,0},{2,1},{3,2},{4,3},{5,4},{6,5},{7,6},{8,7},{9,8},{10,9},{11,1... | collective-permute-start | bytes 4423688 | tf_op jit(solution)/shard_map/ppermute | solution.py:87
  56.5 48.8 %collective-permute-start = (bf16[1440,512]{1,0:T(8,128)(2,1)}, bf16[1440,512]{1,0:T(8,128)(2,1)}, u32[]{:S(2)}, u32[]{:S(2)}) collective-permute-start(bf16[1440,512]{1,0:T(8,128)(2,1)} %bitcast.35), channel_id=1, source_target_pairs={{0,1},{1,2},{2,3},{3,4},{4,5},{5,6},{6,7},{7,8},{8,9},{9,10},{10,1... | collective-permute-start | bytes 4423688 | tf_op jit(solution)/shard_map/ppermute | solution.py:87
  60.1 1.4 copy-start.4
  79.1 49.1 %collective-permute-start.2 = (bf16[1440,512]{1,0:T(8,128)(2,1)}, bf16[1440,512]{1,0:T(8,128)(2,1)}, u32[]{:S(2)}, u32[]{:S(2)}) collective-permute-start(bf16[1440,512]{1,0:T(8,128)(2,1)} %get-tuple-element.10), channel_id=1, source_target_pairs={{1,0},{2,1},{3,2},{4,3},{5,4},{6,5},{7,6},{8,7},{9,8},{10,9},{11,1... | collective-permute-start | bytes 4423688 | tf_op jit(solution)/shard_map/ppermute | solution.py:87
  81.2 47.1 %collective-permute-start.3 = (bf16[1440,512]{1,0:T(8,128)(2,1)}, bf16[1440,512]{1,0:T(8,128)(2,1)}, u32[]{:S(2)}, u32[]{:S(2)}) collective-permute-start(bf16[1440,512]{1,0:T(8,128)(2,1)} %get-tuple-element.11), channel_id=1, source_target_pairs={{0,1},{1,2},{2,3},{3,4},{4,5},{5,6},{6,7},{7,8},{8,9},{9,10},{10,1... | collective-permute-start | bytes 4423688 | tf_op jit(solution)/shard_map/ppermute | solution.py:87
  105.3 1.4 copy-start.2
Sparse Core Ops, SparseCore 0:
  128.3 76.1 reduce-scatter.1

commit v2 on v1

v2 whole, which is shorter than its diff:
```python
import functools

import jax
import jax.numpy as jnp
from jax import lax
from jax.experimental import pallas as pl
from jax.experimental.pallas import tpu as pltpu
from jax.sharding import PartitionSpec as P

F32 = jnp.float32
BF16 = jnp.bfloat16


def spread_columns(channels, kernels, dtype):
    size = channels * kernels
    row = lax.broadcasted_iota(jnp.int32, (size, size), 0)
    col = lax.broadcasted_iota(jnp.int32, (size, size), 1)
    return ((row % channels) * kernels + row // channels == col).astype(dtype)


def fused_kernel(kernels, block, slots, sections, to_ref, from_ref, fields_ref, cot_t_ref, cot_ref, mix_ref, wa_ref, wf_ref,
                 mixed_ref, fg_ref, grad_ref,
                 rows_ref, x_ref, gf_ref, a0_ref, a1_ref, a2_ref, h0_ref, h2_ref, band_ref,
                 part_ref, pair_ref, sum_ref, got_ref,
                 f_send, f_recv, x_send, x_recv, h_send, h_recv, b_send, b_recv, p_send, p_recv, g_send, g_recv):
    width, channels = cot_t_ref.shape
    nblocks = width // block
    n, per_device, _ = fields_ref.shape
    tile = 128
    groups = channels // tile
    per_group = tile // per_device
    me = lax.axis_index("lon")
    core = lax.rem(me, 2)
    pair = me + 1 - 2 * core
    cols = lambda k: slice(k * channels, (k + 1) * channels)
    has_prev, has_next = me > 0, me < n - 1

    def remote(src, dst, send, recv, device):
        return pltpu.make_async_remote_copy(
            src_ref=src, dst_ref=dst, send_sem=send, recv_sem=recv,
            device_id={"lon": device}, device_id_type=pl.DeviceIdType.MESH)

    def peer_of(i):
        return lax.rem(me + i, n)

    barrier = pltpu.get_barrier_semaphore()

    @pl.loop(1, n)
    def _(i):
        pl.semaphore_signal(barrier, inc=1, device_id={"lon": peer_of(i)}, device_id_type=pl.DeviceIdType.MESH)
    pl.semaphore_wait(barrier, n - 1)

    def field_copy(i):
        peer = peer_of(i)
        return remote(fields_ref.at[peer], rows_ref.at[me], f_send.at[i], f_recv.at[me], peer)

    @pl.loop(1, n)
    def _(i):
        field_copy(i).start()
    rows_ref[me] = fields_ref[me]

    @pl.when(jnp.logical_not(has_prev))
    def _():
        x_ref[0] = jnp.zeros((nblocks, block, channels), BF16)
        h2_ref[...] = jnp.zeros((width, channels), BF16)

    @pl.when(jnp.logical_not(has_next))
    def _():
        x_ref[2] = jnp.zeros((nblocks, block, channels), BF16)
        h0_ref[...] = jnp.zeros((width, channels), BF16)

    some = nblocks // 5
    rows = some * block

    @pl.loop(0, 5)
    def _(step):
        at = pl.ds(pl.multiple_of(step * rows, rows), rows)
        for k in range(kernels):
            gf_ref[pl.ds(step * some, some), :, cols(k)] = jnp.dot(
                cot_t_ref[at, :], mix_ref[:, cols(k)], preferred_element_type=F32
            ).astype(BF16).reshape(some, block, channels)

    piece = width // sections

    def down_copy(t):
        at = slice(t * piece, (t + 1) * piece)
        return remote(a0_ref.at[at], h0_ref.at[at], h_send.at[0, t], h_recv.at[0, t], me - 1)

    def up_copy(t):
        at = slice(t * piece, (t + 1) * piece)
        return remote(a2_ref.at[at], h2_ref.at[at], h_send.at[1, t], h_recv.at[1, t], me + 1)

    for t in range(sections):
        @pl.loop(t * (nblocks // sections), (t + 1) * (nblocks // sections))
        def _(b):
            parts = []
            for s in range(slots):
                found = gf_ref[from_ref[s, b]]
                for k in range(kernels):
                    parts.append(found[:, cols(k)])
            out = jnp.dot(wa_ref[...], jnp.concatenate(parts, axis=0), preferred_element_type=F32)
            at = pl.ds(pl.multiple_of(b * block, block), block)
            a0_ref[at, :] = out[:block].astype(BF16)
            a1_ref[at, :] = out[block:2 * block] + cot_t_ref[at, :].astype(F32)
            a2_ref[at, :] = out[2 * block:].astype(BF16)

        @pl.when(has_prev)
        def _():
            down_copy(t).start()

        @pl.when(has_next)
        def _():
            up_copy(t).start()

    def row_copy(to_next, g):
        at = (slice(None), slice(None), slice(g * tile, (g + 1) * tile))
        which, device = (0, me + 1) if to_next else (2, me - 1)
        return remote(x_ref.at[(1,) + at], x_ref.at[(which,) + at],
                      x_send.at[which // 2, g], x_recv.at[which // 2, g], device)

    for g in range(groups):
        @pl.loop(g * per_group, (g + 1) * per_group)
        def _(j):
            @pl.when(j != me)
            def _():
                remote(fields_ref.at[j], rows_ref.at[j], f_send.at[0], f_recv.at[j], pair).wait_recv()
        for start in range(0, width, tile):
            stop = min(start + tile, width)
            x_ref[1, start // block:stop // block, :, g * tile:(g + 1) * tile] = rows_ref[
                g * per_group:(g + 1) * per_group, :, start:stop
            ].reshape(tile, stop - start).T.reshape((stop - start) // block, block, tile)

        @pl.when(has_next)
        def _():
            row_copy(True, g).start()

        @pl.when(has_prev)
        def _():
            row_copy(False, g).start()

    for t in range(sections):
        @pl.when(has_next)
        def _():
            down_copy(t).wait_recv()

        @pl.when(has_prev)
        def _():
            up_copy(t).wait_recv()
    for start in range(0, width, tile):
        stop = min(start + tile, width)
        total = (a1_ref[start:stop] + h0_ref[start:stop].astype(F32) + h2_ref[start:stop].astype(F32)).astype(BF16)
        band_ref[:, :, start:stop] = total.T.reshape(n, per_device, stop - start)

    def band_copy(i):
        peer = peer_of(i)
        return remote(band_ref.at[peer], fg_ref.at[me], b_send.at[i], b_recv.at[me], peer)

    @pl.loop(1, n)
    def _(i):
        band_copy(i).start()
    fg_ref[me] = band_ref[me]

    for g in range(groups):
        @pl.when(has_prev)
        def _():
            row_copy(True, g).wait_recv()

        @pl.when(has_next)
        def _():
            row_copy(False, g).wait_recv()

    @pl.loop(0, nblocks)
    def _(b):
        parts = []
        for s in range(slots):
            for d in range(3):
                parts.append(x_ref[d, to_ref[s, b]])
        out = jnp.dot(wf_ref[...], jnp.concatenate(parts, axis=0), preferred_element_type=F32).astype(BF16)
        for k in range(kernels):
            gf_ref[b, :, cols(k)] = out[k * block:(k + 1) * block]

    half = channels // 2

    def pair_copy(k):
        return remote(part_ref.at[k, 1 - core], pair_ref.at[k], p_send.at[k], p_recv.at[k], pair)

    for k in range(kernels):
        part_ref[k] = jnp.dot(
            cot_ref[...], gf_ref[:, :, cols(k)].reshape(width, channels), preferred_element_type=F32
        ).reshape(2, half, channels)
        pair_copy(k).start()

    @pl.loop(0, 5)
    def _(step):
        at = pl.ds(pl.multiple_of(step * rows, rows), rows)
        blocks = pl.ds(step * some, some)
        mixed = lax.dot_general(
            gf_ref[blocks].reshape(rows, kernels * channels), mix_ref[...],
            (((1,), (1,)), ((), ())), preferred_element_type=F32)
        mixed_ref[at, :] = (x_ref[1, blocks].reshape(rows, channels).astype(F32) + mixed).astype(BF16)

    chips = n // 2
    chip = me // 2
    for k in range(kernels):
        pair_copy(k).wait_recv()
        sum_ref[:, :, cols(k)] = (part_ref[k, core] + pair_ref[k]).astype(BF16).reshape(chips, per_device, channels)

    def sum_copy(i):
        peer = lax.rem(chip + i, chips)
        return remote(sum_ref.at[peer], got_ref.at[chip], g_send.at[i], g_recv.at[chip], 2 * peer + core)

    @pl.loop(1, chips)
    def _(i):
        sum_copy(i).start()
    own = pl.ds(pl.multiple_of(chip * per_device, per_device), per_device)
    for k in range(kernels):
        grad_ref[:, cols(k)] = part_ref[k, core, own, :] + pair_ref[k, own, :]

    @pl.loop(1, chips)
    def _(i):
        j = lax.rem(chip + i, chips)
        remote(sum_ref.at[j], got_ref.at[j], g_send.at[0], g_recv.at[j], pair).wait_recv()
        grad_ref[...] += got_ref[j].astype(F32)
        sum_copy(i).wait_send()

    @pl.loop(1, n)
    def _(i):
        j = peer_of(i)
        remote(band_ref.at[j], fg_ref.at[j], b_send.at[0], b_recv.at[j], pair).wait_recv()
        band_copy(i).wait_send()
        field_copy(i).wait_send()
    for k in range(kernels):
        pair_copy(k).wait_send()

    @pl.when(has_next)
    def _():
        for t in range(sections):
            up_copy(t).wait_send()
        for g in range(groups):
            row_copy(True, g).wait_send()

    @pl.when(has_prev)
    def _():
        for t in range(sections):
            down_copy(t).wait_send()
        for g in range(groups):
            row_copy(False, g).wait_send()


def local(fields, filter_basis, offsets, counts, mixing, cotangent):
    channels, columns = mixing.shape
    kernels = columns // channels
    _, taps, slots, block, outer = filter_basis.shape
    width = fields.shape[2]
    n = lax.axis_size("lon")
    per_device = channels // n
    groups = channels // 128
    sections = 3
    vmem = pl.BlockSpec(memory_space=pltpu.VMEM)
    smem = pl.BlockSpec(memory_space=pltpu.SMEM)

    live = jnp.arange(slots) < counts[0]
    basis = jnp.where(live[None, :, None, None], filter_basis[0], 0)
    w_adj = basis.transpose(0, 2, 1, 3).reshape(taps * block, slots * outer)
    w_fwd = basis.transpose(3, 1, 0, 2).reshape(outer, slots * taps * block)
    nblocks = width // block
    at = jnp.arange(nblocks, dtype=jnp.int32)[None, :]
    to = (at + offsets[0][:, None]) % nblocks
    source = (at - offsets[0][:, None]) % nblocks
    perm = spread_columns(channels, kernels, BF16)
    mix = lax.dot_general(mixing, perm, (((1,), (1,)), ((), ())), preferred_element_type=F32).astype(BF16)
    cot_t = cotangent[:, 0, :].T
    cot = cotangent.reshape(n // 2, 2, per_device, width).transpose(1, 0, 2, 3).reshape(channels, width)

    wide = (width, channels)
    dma = pltpu.SemaphoreType.DMA
    mixed_t, fg, grad = pl.pallas_call(
        functools.partial(fused_kernel, kernels, block, slots, sections),
        out_shape=[
            jax.ShapeDtypeStruct(wide, BF16),
            jax.ShapeDtypeStruct((n, per_device, width), BF16),
            jax.ShapeDtypeStruct((per_device, columns), F32),
        ],
        in_specs=[smem] * 2 + [vmem] * 6,
        out_specs=[vmem] * 3,
        scratch_shapes=[
            pltpu.VMEM((n, per_device, width), BF16),
            pltpu.VMEM((taps, width // block, block, channels), BF16),
            pltpu.VMEM((width // block, block, columns), BF16),
            pltpu.VMEM(wide, BF16),
            pltpu.VMEM(wide, F32),
            pltpu.VMEM(wide, BF16),
            pltpu.VMEM(wide, BF16),
            pltpu.VMEM(wide, BF16),
            pltpu.VMEM((n, per_device, width), BF16),
            pltpu.VMEM((kernels, 2, channels // 2, channels), F32),
            pltpu.VMEM((kernels, channels // 2, channels), F32),
            pltpu.VMEM((n // 2, per_device, columns), BF16),
            pltpu.VMEM((n // 2, per_device, columns), BF16),
            dma((n,)), dma((n,)),
            dma((2, groups)), dma((2, groups)),
            dma((2, sections)), dma((2, sections)),
            dma((n,)), dma((n,)),
            dma((kernels,)), dma((kernels,)),
            dma((n // 2,)), dma((n // 2,)),
        ],
        compiler_params=pltpu.CompilerParams(
            collective_id=0, has_side_effects=True, vmem_limit_bytes=56 * 2**20),
        cost_estimate=pl.CostEstimate(flops=6 * 10**10, bytes_accessed=10**7, transcendentals=0),
        name="fused",
    )(to, source, fields.transpose(1, 0, 2), cot_t, cot, mix, w_adj, w_fwd)
    grad = lax.dot(grad, spread_columns(channels, kernels, F32), precision=lax.Precision.HIGHEST)
    return mixed_t.T[:, None, :], fg.transpose(1, 0, 2), grad


def solution(mesh):
    in_specs = (
        P(("grp", "lon"), None, None),
        P("lon", None, None, None, None),
        P("lon", None),
        P("lon"),
        P(),
        P("grp", "lon", None),
    )
    out_specs = (P("grp", "lon", None), P(("grp", "lon"), None, None), P(("grp", "lon"), None))
    return jax.shard_map(local, mesh=mesh, in_specs=in_specs, out_specs=out_specs, check_vma=False)
```

time: 221 us -> 167 us (0.76); the launches traced: 217 us -> 166 us
  Pallas kernels: 39.2 us -> 141 us
  waiting for transfers between devices: 59.3 us -> 0 us
  blocking collectives: 56 us -> 0 us
  starting transfers between devices: 17 us -> 0 us
  between operations: 14.8 us -> 1.46 us
  local copies, waits for them, and re-layouts: 14.7 us -> 11.2 us
    pallas_call x2 -> x1, Pallas kernels: 39.2 us -> 141 us  [local(): pl.pallas_call(functools.partial(fused_kernel, kernels, block, slots, sec...]
    all_to_all x1 -> x0, blocking collectives: 56 us -> none  [local(): lax.all_to_all(banded, 'lon', split_axis=0, concat_axis=0, tiled=True)]
    all_to_all x1 -> x0, waiting for transfers between devices: 28.2 us -> none  [local(): lax.all_to_all(fields.transpose(1, 0, 2), 'lon', split_axis=0, concat_axi...]
    ppermute x4 -> x0, waiting for transfers between devices: 18.9 us -> none  [passed_along(): lax.ppermute(value, axis, [(source, source + steps) for source in range(l...]
    reduce_scatter x1 -> x0, waiting for transfers between devices: 12.2 us -> none  [local(): grad = lax.psum_scatter(grad, 'lon', scatter_dimension=0, tiled=True)]
    ppermute x4 -> x0, starting transfers between devices: 10.8 us -> none  [passed_along(): lax.ppermute(value, axis, [(source, source + steps) for source in range(l...]
    all_to_all x1 -> x0, starting transfers between devices: 6.15 us -> none  [local(): lax.all_to_all(fields.transpose(1, 0, 2), 'lon', split_axis=0, concat_axi...]
    transpose x2 -> x1, other arithmetic: 4.52 us -> 1 us  [local(): w_fwd = basis.transpose(3, 1, 0, 2).reshape(outer, slots * taps * block)]
  transfers between devices with their start and end apart: 6 -> 0, of which waited for: 3 -> 0; matrix products, arithmetic and copies ran while one was open for 7% -> 0% of each run, Pallas kernels for 18% -> 0%
where the time goes in v2:
time: 167 us; the launch traced here: 166 us
  Pallas kernels  141 us (84%)
  local copies, waits for them, and re-layouts  11.2 us (7%)
  matrix products  10.3 us (6%)
  other arithmetic  2.36 us (1%)
    pallas_call x1, Pallas kernels, local(): pl.pallas_call(functools.partial(fused_kernel, kernels, block, slots, sec...  141 us
    unnamed x12, local copies, waits for them, and re-layouts  8.29 us
    dot_general x1, matrix products, local(): lax.dot_general(mixing, perm, (((1,), (1,)), ((), ())), preferred_element...  5.88 us
    dot_general x1, matrix products, local(): lax.dot(grad, spread_columns(channels, kernels, F32), precision=lax.Preci...  4.43 us

profile of v2, /device:TPU:28, one launch (start us, length us, event | category | flops | bytes accessed | tf_op | source)
XLA Modules:
  0.0 166.3 jit_solution(14379653809911916757)
XLA Ops:
  0.6 0.0 copy-start
  1.4 1.3 add_select_fusion
  2.8 1.0 fusion.1
  3.8 0.8 copy.21.wf_ref
  4.6 0.1 copy.19
  4.7 0.8 reshape.25.wa_ref
  5.5 0.0 copy-done
  5.5 0.0 copy-start.1
  5.5 5.9 %fusion.mix_ref = bf16[512,1536]{1,0:T(8,128)(2,1)} fusion(bf16[512,1536]{1,0:T(8,128)(2,1)S(1)} %copy-done, s32[1536]{0:T(1024)S(1)} %get-tuple-element.19, s32[1536]{0:T(1024)S(1)} %get-tuple-element.22, s32[1536]{0:T(1024)S(1)} %get-tuple-element.20, s32[1536]{0:T(1024)S(1)} %get-tuple-element.21, pred[1536]{0:T(1024)(128)(4,1)S(1)} %get-tuple-element.23, ...), kind=kOutput, calls=%fused_computation.2 | convolution fusion | flops 2428502016 | bytes 3173376 | tf_op jit(solution)/shard_map/dot_general | solution.py:271
  11.4 0.0 copy-done.1
  11.4 2.0 %copy.25 = bf16[32,16,1440]{2,0,1:T(8,128)(2,1)} copy(bf16[32,16,1440]{2,1,0:T(8,128)(2,1)S(1)} %copy-done.1) | data formatting | bytes 2949120 | tf_op args[0]
  13.4 1.7 %copy.16 = bf16[512,1,1440]{2,0,1:T(8,128)(2,1)S(1)} copy(bf16[512,1,1440]{0,2,1:T(8,128)(2,1)} %param.11) | data formatting | bytes 2949120 | tf_op args[5]
  15.1 1.3 copy.17
  16.3 140.9 %fused.1 = (bf16[1440,512]{1,0:T(8,128)(2,1)}, bf16[16,32,1440]{2,1,0:T(8,128)(2,1)}, f32[32,1536]{1,0:T(8,128)}) custom-call(s32[6,45]{1,0:T(8,128)} %get-tuple-element.18.to_ref, s32[6,45]{1,0:T(8,128)} %get-tuple-element.17.from_ref, bf16[16,32,1440]{2,1,0:T(8,128)(2,1)} %bitcast.33, bf16[1440,512]{1,0:T(8,128)(2,1)} %bitcast.36, ...), custom_call_target="tpu_custom_call" | custom-call | flops 60000002048 | bytes 10000000 | tf_op jit(solution)/shard_map/fused/pallas_call | solution.py:277
  157.3 0.0 copy-start.3
  157.3 3.5 %copy.22 = bf16[32,16,1440]{2,1,0:T(8,128)(2,1)} copy(bf16[32,16,1440]{2,0,1:T(8,128)(2,1)} %bitcast.35) | data formatting | bytes 2949120
  160.8 0.0 copy-done.3
  160.8 0.0 copy-start.2
  160.8 4.4 %fusion.15 = f32[32,1536]{1,0:T(8,128)} fusion(f32[32,1536]{1,0:T(8,128)S(1)} %copy-done.3, s32[1536]{0:T(1024)S(1)} %get-tuple-element.19, s32[1536]{0:T(1024)S(1)} %get-tuple-element.22, s32[1536]{0:T(1024)S(1)} %get-tuple-element.20, s32[1536]{0:T(1024)S(1)} %get-tuple-element.21, pred[1536]{0:T(1024)(128)(4,1)S(1)} %get-tuple-element.23, ...), kind=kOutput, calls=%fused_computation.28 | convolution fusion | flops 917766144 | bytes 420864 | tf_op jit(solution)/shard_map/dot_general | solution.py:312
  165.2 0.0 copy-done.2
  165.2 1.1 copy.28
  (5 shorter events, 0.0 us)
Async XLA Ops:
  0.6 4.8 %copy-start = (bf16[512,1536]{1,0:T(8,128)(2,1)S(1)}, bf16[512,1536]{1,0:T(8,128)(2,1)}, u32[]{:S(2)}) copy-start(bf16[512,1536]{1,0:T(8,128)(2,1)} %param.10) | copy-start | bytes 4718596
  5.5 5.9 %copy-start.1 = (bf16[32,16,1440]{2,1,0:T(8,128)(2,1)S(1)}, bf16[32,16,1440]{2,1,0:T(8,128)(2,1)}, u32[]{:S(2)}) copy-start(bf16[32,16,1440]{2,1,0:T(8,128)(2,1)} %param.6) | copy-start | bytes 4423684
  157.3 3.5 %copy-start.3 = (f32[32,1536]{1,0:T(8,128)S(1)}, f32[32,1536]{1,0:T(8,128)}, u32[]{:S(2)}) copy-start(f32[32,1536]{1,0:T(8,128)} %get-tuple-element.8) | copy-start | bytes 589828
  160.8 4.4 %copy-start.2 = (bf16[1440,512]{1,0:T(8,128)(2,1)S(1)}, bf16[1440,512]{1,0:T(8,128)(2,1)}, u32[]{:S(2)}) copy-start(bf16[1440,512]{1,0:T(8,128)(2,1)} %get-tuple-element.6) | copy-start | bytes 4423684

commit v3 on v2

--- a/solution.py
+++ b/solution.py
@@ -18,9 +18,9 @@
     return ((row % channels) * kernels + row // channels == col).astype(dtype)
 
 
-def fused_kernel(kernels, block, slots, sections, to_ref, from_ref, fields_ref, cot_t_ref, cot_ref, mix_ref, wa_ref, wf_ref,
+def fused_kernel(kernels, block, slots, sections, to_ref, from_ref, live_ref, fields_ref, cot_t_ref, mixing_ref, basis_ref,
                  mixed_ref, fg_ref, grad_ref,
-                 rows_ref, x_ref, gf_ref, a0_ref, a1_ref, a2_ref, h0_ref, h2_ref, band_ref,
+                 mix_ref, cot_ref, wa_ref, wf_ref, rows_ref, x_ref, gf_ref, a0_ref, a1_ref, a2_ref, h0_ref, h2_ref, band_ref,
                  part_ref, pair_ref, sum_ref, got_ref,
                  f_send, f_recv, x_send, x_recv, h_send, h_recv, b_send, b_recv, p_send, p_recv, g_send, g_recv):
     width, channels = cot_t_ref.shape
@@ -69,6 +69,20 @@
         x_ref[2] = jnp.zeros((nblocks, block, channels), BF16)
         h0_ref[...] = jnp.zeros((width, channels), BF16)
 
+    row = lax.broadcasted_iota(jnp.int32, (kernels * channels, channels), 0)
+    col = lax.broadcasted_iota(jnp.int32, (kernels * channels, channels), 1)
+    for k in range(kernels):
+        pick = jnp.where(row == kernels * col + k, 1.0, 0.0).astype(BF16)
+        mix_ref[:, cols(k)] = jnp.dot(mixing_ref[...], pick, preferred_element_type=F32).astype(BF16)
+    taps = basis_ref.shape[0]
+    outer = kernels * block
+    for s in range(slots):
+        for d in range(taps):
+            piece = basis_ref[d, s].astype(F32) * live_ref[s]
+            wa_ref[d * block:(d + 1) * block, s * outer:(s + 1) * outer] = piece.astype(BF16)
+            at = (s * taps + d) * block
+            wf_ref[:, at:at + block] = piece.T.astype(BF16)
+
     some = nblocks // 5
     rows = some * block
 
@@ -112,6 +126,10 @@
         def _():
             up_copy(t).start()
 
+    for start in range(0, width, tile):
+        stop = min(start + tile, width)
+        cot_ref[:, start:stop] = cot_t_ref[start:stop, :].T
+
     def row_copy(to_next, g):
         at = (slice(None), slice(None), slice(g * tile, (g + 1) * tile))
         which, device = (0, me + 1) if to_next else (2, me - 1)
@@ -179,15 +197,16 @@
         for k in range(kernels):
             gf_ref[b, :, cols(k)] = out[k * block:(k + 1) * block]
 
-    half = channels // 2
+    chips = n // 2
+    chip = me // 2
 
     def pair_copy(k):
-        return remote(part_ref.at[k, 1 - core], pair_ref.at[k], p_send.at[k], p_recv.at[k], pair)
+        return remote(part_ref.at[k, :, 1 - core], pair_ref.at[k], p_send.at[k], p_recv.at[k], pair)
 
     for k in range(kernels):
         part_ref[k] = jnp.dot(
             cot_ref[...], gf_ref[:, :, cols(k)].reshape(width, channels), preferred_element_type=F32
-        ).reshape(2, half, channels)
+        ).reshape(chips, 2, per_device, channels)
         pair_copy(k).start()
 
     @pl.loop(0, 5)
@@ -199,11 +218,9 @@
             (((1,), (1,)), ((), ())), preferred_element_type=F32)
         mixed_ref[at, :] = (x_ref[1, blocks].reshape(rows, channels).astype(F32) + mixed).astype(BF16)
 
-    chips = n // 2
-    chip = me // 2
     for k in range(kernels):
         pair_copy(k).wait_recv()
-        sum_ref[:, :, cols(k)] = (part_ref[k, core] + pair_ref[k]).astype(BF16).reshape(chips, per_device, channels)
+        sum_ref[:, :, cols(k)] = (part_ref[k, :, core] + pair_ref[k]).astype(BF16)
 
     def sum_copy(i):
         peer = lax.rem(chip + i, chips)
@@ -212,9 +229,8 @@
     @pl.loop(1, chips)
     def _(i):
         sum_copy(i).start()
-    own = pl.ds(pl.multiple_of(chip * per_device, per_device), per_device)
-    for k in range(kernels):
-        grad_ref[:, cols(k)] = part_ref[k, core, own, :] + pair_ref[k, own, :]
+    for k in range(kernels):
+        grad_ref[:, cols(k)] = part_ref[k, chip, core] + pair_ref[k, chip]
 
     @pl.loop(1, chips)
     def _(i):
@@ -259,18 +275,12 @@
     vmem = pl.BlockSpec(memory_space=pltpu.VMEM)
     smem = pl.BlockSpec(memory_space=pltpu.SMEM)
 
-    live = jnp.arange(slots) < counts[0]
-    basis = jnp.where(live[None, :, None, None], filter_basis[0], 0)
-    w_adj = basis.transpose(0, 2, 1, 3).reshape(taps * block, slots * outer)
-    w_fwd = basis.transpose(3, 1, 0, 2).reshape(outer, slots * taps * block)
+    live = (jnp.arange(slots) < counts[0]).astype(F32)
     nblocks = width // block
     at = jnp.arange(nblocks, dtype=jnp.int32)[None, :]
     to = (at + offsets[0][:, None]) % nblocks
     source = (at - offsets[0][:, None]) % nblocks
-    perm = spread_columns(channels, kernels, BF16)
-    mix = lax.dot_general(mixing, perm, (((1,), (1,)), ((), ())), preferred_element_type=F32).astype(BF16)
     cot_t = cotangent[:, 0, :].T
-    cot = cotangent.reshape(n // 2, 2, per_device, width).transpose(1, 0, 2, 3).reshape(channels, width)
 
     wide = (width, channels)
     dma = pltpu.SemaphoreType.DMA
@@ -281,9 +291,13 @@
             jax.ShapeDtypeStruct((n, per_device, width), BF16),
             jax.ShapeDtypeStruct((per_device, columns), F32),
         ],
-        in_specs=[smem] * 2 + [vmem] * 6,
+        in_specs=[smem] * 3 + [vmem] * 4,
         out_specs=[vmem] * 3,
         scratch_shapes=[
+            pltpu.VMEM((channels, columns), BF16),
+            pltpu.VMEM((channels, width), BF16),
+            pltpu.VMEM((taps * block, slots * outer), BF16),
+            pltpu.VMEM((outer, slots * taps * block), BF16),
             pltpu.VMEM((n, per_device, width), BF16),
             pltpu.VMEM((taps, width // block, block, channels), BF16),
             pltpu.VMEM((width // block, block, columns), BF16),
@@ -293,8 +307,8 @@
             pltpu.VMEM(wide, BF16),
             pltpu.VMEM(wide, BF16),
             pltpu.VMEM((n, per_device, width), BF16),
-            pltpu.VMEM((kernels, 2, channels // 2, channels), F32),
-            pltpu.VMEM((kernels, channels // 2, channels), F32),
+            pltpu.VMEM((kernels, n // 2, 2, per_device, channels), F32),
+            pltpu.VMEM((kernels, n // 2, per_device, channels), F32),
             pltpu.VMEM((n // 2, per_device, columns), BF16),
             pltpu.VMEM((n // 2, per_device, columns), BF16),
             dma((n,)), dma((n,)),
@@ -305,11 +319,14 @@
             dma((n // 2,)), dma((n // 2,)),
         ],
         compiler_params=pltpu.CompilerParams(
-            collective_id=0, has_side_effects=True, vmem_limit_bytes=56 * 2**20),
+            collective_id=0, has_side_effects=True, vmem_limit_bytes=58 * 2**20),
         cost_estimate=pl.CostEstimate(flops=6 * 10**10, bytes_accessed=10**7, transcendentals=0),
         name="fused",
-    )(to, source, fields.transpose(1, 0, 2), cot_t, cot, mix, w_adj, w_fwd)
-    grad = lax.dot(grad, spread_columns(channels, kernels, F32), precision=lax.Precision.HIGHEST)
+    )(to, source, live, fields.transpose(1, 0, 2), cot_t, mixing, filter_basis[0])
+    high = lax.reduce_precision(grad, exponent_bits=8, mantissa_bits=7)
+    grad = jnp.dot(
+        jnp.concatenate([high, grad - high]).astype(BF16), spread_columns(channels, kernels, BF16), preferred_element_type=F32)
+    grad = grad[:per_device] + grad[per_device:]
     return mixed_t.T[:, None, :], fg.transpose(1, 0, 2), grad
 
 

time: 167 us -> 155 us (0.928)
  matrix products: 10.3 us -> 2.35 us
  local copies, waits for them, and re-layouts: 11.2 us -> 6.54 us
    dot_general x2 -> x1, matrix products: 10.3 us -> 2.35 us  [local(): jnp.dot(jnp.concatenate([high, grad - high]).astype(BF16), spread_columns...]
    unnamed x12 -> x7, local copies, waits for them, and re-layouts: 8.29 us -> 6.54 us
where the time goes in v3:
time: 155 us
  Pallas kernels  141 us (91%)
  local copies, waits for them, and re-layouts  6.54 us (4%)
  other arithmetic  3.54 us (2%)
  matrix products  2.35 us (2%)
    pallas_call x1, Pallas kernels, local(): pl.pallas_call(functools.partial(fused_kernel, kernels, block, slots, sec...  141 us
    unnamed x7, local copies, waits for them, and re-layouts  6.54 us

profile of v3, /device:TPU:28, one launch (start us, length us, event | category | flops | bytes accessed | tf_op | source)
XLA Modules:
  0.0 154.6 jit_solution(13028926407543924556)
XLA Ops:
  0.6 1.3 add_select_fusion
  2.0 3.4 %copy.12 = bf16[32,16,1440]{2,0,1:T(8,128)(2,1)} copy(bf16[32,16,1440]{2,1,0:T(8,128)(2,1)} %param.6) | data formatting | bytes 2949120 | tf_op args[0]
  6.0 0.5 compare_convert_fusion.live_ref
  6.6 140.8 %fused.1 = (bf16[1440,512]{1,0:T(8,128)(2,1)}, bf16[16,32,1440]{2,1,0:T(8,128)(2,1)}, f32[32,1536]{1,0:T(8,128)}) custom-call(s32[6,45]{1,0:T(8,128)} %get-tuple-element.15.to_ref, s32[6,45]{1,0:T(8,128)} %get-tuple-element.14.from_ref, f32[6]{0:T(128)} %compare_convert_fusion.live_ref, bf16[16,32,1440]{2,1,0:T(8,128)(2,1)} %bitcast.15, ...), custom_call_target="tpu_custom_call" | custom-call | flops 60000002048 | bytes 10000000 | tf_op jit(solution)/shard_map/fused/pallas_call | solution.py:287
  147.4 1.0 reduce-precision_convert_fusion
  148.4 0.0 copy-start
  148.4 2.4 %fusion = f32[64,1536]{1,0:T(8,128)S(1)} fusion(s32[1536]{0:T(1024)S(1)} %get-tuple-element.16, s32[1536]{0:T(1024)S(1)} %get-tuple-element.19, s32[1536]{0:T(1024)S(1)} %get-tuple-element.17, s32[1536]{0:T(1024)S(1)} %get-tuple-element.18, pred[1536]{0:T(1024)(128)(4,1)S(1)} %get-tuple-element.20, pred[1536]{0:T(1024)(128)(4,1)S(1)} %get-tuple-element.21, ...), kind=kOutput, calls=%fused_computation.1 | convolution fusion | flops 314179584 | bytes 617472 | tf_op jit(solution)/shard_map/dot_general | solution.py:327
  150.8 0.7 slice_add_fusion
  151.5 0.0 copy-done
  151.5 0.0 copy-start.1
  151.5 2.0 %copy.10 = bf16[32,16,1440]{2,1,0:T(8,128)(2,1)} copy(bf16[32,16,1440]{2,0,1:T(8,128)(2,1)S(1)} %bitcast.14) | data formatting | bytes 2949120
  153.5 0.0 copy-done.1
  153.5 1.1 copy.15
  (3 shorter events, 0.0 us)
Async XLA Ops:
  148.4 3.1 %copy-start = (bf16[16,32,1440]{2,1,0:T(8,128)(2,1)S(1)}, bf16[16,32,1440]{2,1,0:T(8,128)(2,1)}, u32[]{:S(2)}) copy-start(bf16[16,32,1440]{2,1,0:T(8,128)(2,1)} %get-tuple-element.7) | copy-start | bytes 4423684
  151.5 2.0 %copy-start.1 = (bf16[1440,512]{1,0:T(8,128)(2,1)S(1)}, bf16[1440,512]{1,0:T(8,128)(2,1)}, u32[]{:S(2)}) copy-start(bf16[1440,512]{1,0:T(8,128)(2,1)} %get-tuple-element.6) | copy-start | bytes 4423684

commit v4 on v3

--- a/solution.py
+++ b/solution.py
@@ -130,22 +130,29 @@
         stop = min(start + tile, width)
         cot_ref[:, start:stop] = cot_t_ref[start:stop, :].T
 
+    def lanes(g):
+        return pl.ds(g * tile if isinstance(g, int) else pl.multiple_of(g * tile, tile), tile)
+
     def row_copy(to_next, g):
-        at = (slice(None), slice(None), slice(g * tile, (g + 1) * tile))
+        at = (slice(None), slice(None), lanes(g))
         which, device = (0, me + 1) if to_next else (2, me - 1)
         return remote(x_ref.at[(1,) + at], x_ref.at[(which,) + at],
                       x_send.at[which // 2, g], x_recv.at[which // 2, g], device)
 
-    for g in range(groups):
-        @pl.loop(g * per_group, (g + 1) * per_group)
-        def _(j):
+    for turn in range(groups):
+        g = lax.rem(me // per_group + turn, groups)
+
+        @pl.loop(0, per_group)
+        def _(i):
+            j = g * per_group + i
+
             @pl.when(j != me)
             def _():
                 remote(fields_ref.at[j], rows_ref.at[j], f_send.at[0], f_recv.at[j], pair).wait_recv()
         for start in range(0, width, tile):
             stop = min(start + tile, width)
-            x_ref[1, start // block:stop // block, :, g * tile:(g + 1) * tile] = rows_ref[
-                g * per_group:(g + 1) * per_group, :, start:stop
+            x_ref[1, start // block:stop // block, :, lanes(g)] = rows_ref[
+                pl.ds(g * per_group, per_group), :, start:stop
             ].reshape(tile, stop - start).T.reshape((stop - start) // block, block, tile)
 
         @pl.when(has_next)

time: 155 us -> 155 us (level)
  no operation moved by 1% of the time
where the time goes in v4:
time: 155 us
  Pallas kernels  141 us (91%)
  local copies, waits for them, and re-layouts  6.54 us (4%)
  other arithmetic  3.54 us (2%)
  matrix products  2.35 us (2%)
    pallas_call x1, Pallas kernels, local(): pl.pallas_call(functools.partial(fused_kernel, kernels, block, slots, sec...  141 us
    unnamed x7, local copies, waits for them, and re-layouts  6.54 us

profile of v4, /device:TPU:28, one launch (start us, length us, event | category | flops | bytes accessed | tf_op | source)
XLA Modules:
  0.0 154.6 jit_solution(2775659948585892025)
XLA Ops:
  0.6 1.3 add_select_fusion
  2.0 3.4 %copy.12 = bf16[32,16,1440]{2,0,1:T(8,128)(2,1)} copy(bf16[32,16,1440]{2,1,0:T(8,128)(2,1)} %param.6) | data formatting | bytes 2949120 | tf_op args[0]
  6.0 0.5 compare_convert_fusion.live_ref
  6.6 140.8 %fused.1 = (bf16[1440,512]{1,0:T(8,128)(2,1)}, bf16[16,32,1440]{2,1,0:T(8,128)(2,1)}, f32[32,1536]{1,0:T(8,128)}) custom-call(s32[6,45]{1,0:T(8,128)} %get-tuple-element.15.to_ref, s32[6,45]{1,0:T(8,128)} %get-tuple-element.14.from_ref, f32[6]{0:T(128)} %compare_convert_fusion.live_ref, bf16[16,32,1440]{2,1,0:T(8,128)(2,1)} %bitcast.15, ...), custom_call_target="tpu_custom_call" | custom-call | flops 60000002048 | bytes 10000000 | tf_op jit(solution)/shard_map/fused/pallas_call | solution.py:294
  147.4 1.0 reduce-precision_convert_fusion
  148.4 0.0 copy-start
  148.4 2.4 %fusion = f32[64,1536]{1,0:T(8,128)S(1)} fusion(s32[1536]{0:T(1024)S(1)} %get-tuple-element.16, s32[1536]{0:T(1024)S(1)} %get-tuple-element.19, s32[1536]{0:T(1024)S(1)} %get-tuple-element.17, s32[1536]{0:T(1024)S(1)} %get-tuple-element.18, pred[1536]{0:T(1024)(128)(4,1)S(1)} %get-tuple-element.20, pred[1536]{0:T(1024)(128)(4,1)S(1)} %get-tuple-element.21, ...), kind=kOutput, calls=%fused_computation.1 | convolution fusion | flops 314179584 | bytes 617472 | tf_op jit(solution)/shard_map/dot_general | solution.py:334
  150.8 0.7 slice_add_fusion
  151.5 0.0 copy-done
  151.5 0.0 copy-start.1
  151.5 2.0 %copy.10 = bf16[32,16,1440]{2,1,0:T(8,128)(2,1)} copy(bf16[32,16,1440]{2,0,1:T(8,128)(2,1)S(1)} %bitcast.14) | data formatting | bytes 2949120
  153.5 0.0 copy-done.1
  153.5 1.1 copy.15
  (3 shorter events, 0.0 us)
Async XLA Ops:
  148.4 3.1 %copy-start = (bf16[16,32,1440]{2,1,0:T(8,128)(2,1)S(1)}, bf16[16,32,1440]{2,1,0:T(8,128)(2,1)}, u32[]{:S(2)}) copy-start(bf16[16,32,1440]{2,1,0:T(8,128)(2,1)} %get-tuple-element.7) | copy-start | bytes 4423684
  151.5 2.0 %copy-start.1 = (bf16[1440,512]{1,0:T(8,128)(2,1)S(1)}, bf16[1440,512]{1,0:T(8,128)(2,1)}, u32[]{:S(2)}) copy-start(bf16[1440,512]{1,0:T(8,128)(2,1)} %get-tuple-element.6) | copy-start | bytes 4423684
